TPU v7x, 32 devices: a whole 2x2x4 slice. The times are simulated.
32 devices in a mesh: wide: 8 (over y, x, core), loop: 4 (over z).
Axes of the slice: x: 2, y: 2, z: 4, core: 2. Of those that a mesh axis runs over, the one named last changes fastest.
Arguments:
- feats: bfloat16 [4096, 512], P('loop'), may hold values from -6 to 6
- tiles: bfloat16 [4, 8, 16, 128, 128], P('loop', 'wide'), may hold values from -0.1875 to 0.1875
- tile_rows: int32 [4, 8, 16], P('loop', 'wide'), may hold values from 0 to 7
- tile_cols: int32 [4, 8, 16], P('loop', 'wide'), may hold values from 0 to 3
- tile_count: int32 [4, 8], P('loop', 'wide'), may hold values from 1 to 16, as said below
- w_msg: bfloat16 [512, 512], replicated, may hold values from -0.25 to 0.25
- w_self: bfloat16 [512, 512], replicated, may hold values from -0.25 to 0.25
- readout: float32 [512], replicated, may hold values from -0.6 to 0.6
- labels: int32 [4096], P('loop'), may hold values from 0 to 1
Outputs:
- logits: float32 [4096], P('loop')
- grad_msg: bfloat16 [512, 512], replicated
- grad_self: bfloat16 [512, 512], replicated
Inputs may be any that keep to these rules, and one draw needn't show every extreme that they name: `tile_count`: some loop and wide index uses all 16 slots in every draw.
All inputs are finite; a program needn't handle non-finite values.
Results may differ from a plain program's by a relative error of at most 0.02.
Values may be sent and summed in bfloat16 or wider, within the bound.
A program may use at most 64 MiB of HBM per device.

v0:
```python
import jax
import jax.numpy as jnp
from jax import lax
from jax.sharding import PartitionSpec as P


def body(feats, tiles, tile_rows, tile_cols, tile_count, w_msg, w_self, readout, labels):
    rows_dev, feat_width = feats.shape
    size_tb = tiles.shape[-1]
    slot_count = tiles.shape[2]
    blocks_dev = rows_dev // size_tb
    wide_size = lax.axis_size("wide")
    cols_own = max(1, blocks_dev // wide_size)
    wide_pos = lax.axis_index("wide")
    picked_blocks = wide_pos % blocks_dev + wide_size * jnp.arange(cols_own, dtype=jnp.int32)
    own_blocks = jnp.take(feats.reshape(blocks_dev, size_tb, feat_width), picked_blocks, axis=0)
    gathered = lax.all_gather(own_blocks, "loop", axis=0, tiled=True)
    tile_vals = tiles.reshape(slot_count, size_tb, size_tb)
    chosen = jnp.take(gathered, tile_cols.reshape(slot_count), axis=0)
    product = jnp.einsum("sij,sjd->sid", tile_vals, chosen, preferred_element_type=jnp.float32)
    valid_slot = jnp.arange(slot_count, dtype=jnp.int32) < tile_count.reshape(())
    placing = (
        (tile_rows.reshape(slot_count)[:, None] == jnp.arange(blocks_dev, dtype=jnp.int32)[None, :])
        & valid_slot[:, None]
    ).astype(jnp.float32)
    partial_value = jnp.einsum(
        "sr,sid->rid", placing, product, precision=lax.Precision.HIGHEST
    ).reshape(rows_dev, feat_width)
    message = lax.psum_scatter(
        partial_value.astype(jnp.bfloat16), "wide", scatter_dimension=0, tiled=True
    )
    share_rows = rows_dev // wide_size
    node_feats = lax.dynamic_slice_in_dim(feats, wide_pos * share_rows, share_rows, 0)
    node_labels = lax.dynamic_slice_in_dim(labels, wide_pos * share_rows, share_rows, 0)
    pre_act = jnp.dot(message, w_msg, preferred_element_type=jnp.float32) + jnp.dot(
        node_feats, w_self, preferred_element_type=jnp.float32
    )
    hidden = node_feats.astype(jnp.float32) + jax.nn.silu(pre_act)
    logits = jnp.dot(hidden, readout, precision=lax.Precision.HIGHEST)
    residual_grad = jax.nn.sigmoid(logits) - node_labels.astype(jnp.float32)
    gate_sig = jax.nn.sigmoid(pre_act)
    pre_grad = (
        residual_grad[:, None] * readout[None, :] * gate_sig * (1.0 + pre_act * (1.0 - gate_sig))
    ).astype(jnp.bfloat16)
    grad_msg = jnp.einsum("na,nb->ab", message, pre_grad, preferred_element_type=jnp.float32)
    grad_self = jnp.einsum("na,nb->ab", node_feats, pre_grad, preferred_element_type=jnp.float32)
    grad_msg, grad_self = lax.psum((grad_msg, grad_self), ("wide", "loop"))
    out_logits = lax.all_gather(logits, "wide", axis=0, tiled=True)
    return (out_logits, grad_msg.astype(jnp.bfloat16), grad_self.astype(jnp.bfloat16))


def solution(mesh):
    placed = (
        P("loop", None),
        P("loop", "wide", None, None, None),
        P("loop", "wide", None),
        P("loop", "wide", None),
        P("loop", "wide"),
        P(),
        P(),
        P(),
        P("loop"),
    )
    return jax.shard_map(
        body, mesh=mesh, in_specs=placed, out_specs=(P("loop"), P(), P()), check_vma=False
    )
```

profile of v0, /device:TPU:1, one launch (start us, length us, event | category | flops | bytes accessed | tf_op | source)
XLA Modules:
  0.0 162.3 jit_solution(1000513786370055912)
XLA Ops:
  7.2 0.0 copy-start
  7.2 0.0 reduce-scatter.2.cloned.1.call-start
  7.2 0.7 fusion.18
  7.9 0.7 compare_and_fusion
  8.6 0.9 dynamic-slice_select_fusion
  9.5 15.3 %all_gather.6 = bf16[4,128,512]{2,1,0:T(8,128)(2,1)S(1)} all-gather(bf16[1,128,512]{2,1,0:T(8,128)(2,1)S(1)} %dynamic-slice_select_fusion), channel_id=1, replica_groups=mesh['wide'=8,'loop'=4] {'loop'}, dimensions={0}, use_global_device_ids=true | all-gather | bytes 655360 | tf_op jit(solution)/shard_map/all_gather | solution.py:17
  24.8 0.7 gather_fusion
  25.5 0.0 copy-done
  25.5 2.8 %convolution_bitcast_fusion = f32[16,128,512]{1,2,0:T(8,128)} fusion(bf16[16,128,512]{2,1,0:T(8,128)(2,1)S(1)} %gather_fusion, pred[16]{0:T(512)(128)(4,1)S(1)} %compare_and_fusion, bf16[1,1,16,128,128]{4,3,2,1,0:T(8,128)(2,1)S(1)} %copy-done), kind=kOutput, calls=%fused_computation.1 | convolution fusion | flops 269484032 | bytes 6815760 | tf_op jit(solution)/shard_map/sij,sjd->sid/dot_general | solution.py:20
  28.3 0.0 copy-start.4
  28.3 5.5 %copy.14 = f32[16,128,512]{2,0,1:T(8,128)} copy(f32[16,128,512]{1,2,0:T(8,128)} %convolution_bitcast_fusion) | data formatting | bytes 8388608 | tf_op jit(solution)/shard_map/sij,sjd->sid/dot_general | solution.py:20
  34.5 0.0 copy-done.4
  34.5 3.8 %convolution_convert_fusion = bf16[8,128,512]{2,0,1:T(8,128)(2,1)S(1)} fusion(f32[16,128,512]{2,0,1:T(8,128)} %copy.14, s32[16]{0:T(128)S(1)} %bitcast.43, pred[16]{0:T(512)(128)(4,1)S(1)} %iota_compare_fusion.1), kind=kOutput, calls=%fused_computation.4 | convolution fusion | flops 101187840 | bytes 5242960 | tf_op jit(solution)/shard_map/sr,sid->rid/dot_general | solution.py:26
  38.3 0.0 copy-start.1
  38.3 0.0 copy-start.2
  38.3 1.3 copy.15
  39.6 0.0 copy-start.5
  39.6 0.0 reduce-scatter.2.cloned.1.call-update
  39.6 39.3 %reduce-scatter.2.cloned.1.call-done = bf16[128,512]{1,0:T(8,128)(2,1)} async-done(((bf16[1024,512]{1,0:T(8,128)(2,1)}), bf16[128,512]{1,0:T(8,128)(2,1)}) %reduce-scatter.2.cloned.1.call-update) | async-done | bytes 131088 | tf_op jit(solution)/shard_map/reduce_scatter | solution.py:29
  78.9 0.0 copy-done.1
  78.9 1.1 fusion.27
  80.0 0.0 copy-done.2
  80.0 0.0 copy-start.3
  80.0 1.2 convolution_add_fusion
  81.2 0.0 copy-done.5
  81.2 1.2 divide_subtract_fusion
  82.5 1.4 fusion.9
  83.8 0.0 copy-done.3
  83.8 0.4 fusion.26
  84.2 9.3 %all-gather = f32[8,1,128]{2,1,0:T(1,128)S(1)} all-gather(f32[1,1,128]{2,1,0:T(1,128)S(1)} %bitcast.44), channel_id=1, replica_groups=mesh['wide'=8,'loop'=4] {'wide'}, dimensions={0}, use_global_device_ids=true | all-gather | bytes 4608 | tf_op jit(solution)/shard_map/all_gather | solution.py:48
  93.5 61.4 %all-reduce.2 = (bf16[512,512]{1,0:T(8,128)(2,1)}, bf16[512,512]{1,0:T(8,128)(2,1)}) all-reduce(f32[512,512]{1,0:T(8,128)S(1)} %fusion.26, f32[512,512]{1,0:T(8,128)S(1)} %fusion.9), channel_id=1, replica_groups=mesh['wide'=8,'loop'=4] {'wide','loop'}, use_global_device_ids=true, to_apply=%region_1.2 | all-reduce | flops 524288 | bytes 3145728 | tf_op jit(solution)/shard_map/psum | solution.py:47
  154.9 0.6 copy.23
  (2 shorter events, 0.0 us)
Async XLA Ops:
  7.2 18.4 %copy-start = (bf16[1,1,16,128,128]{4,3,2,1,0:T(8,128)(2,1)S(1)}, bf16[1,1,16,128,128]{4,3,2,1,0:T(8,128)(2,1)}, u32[]{:S(2)}) copy-start(bf16[1,1,16,128,128]{4,3,2,1,0:T(8,128)(2,1)} %param.10) | copy-start | bytes 1572868
  7.2 71.7 %reduce-scatter.2.cloned.1.call-start = ((), (), s32[]{:S(2)}) async-start(), calls=%async_computation.1 | async-start | bytes 1179648 | tf_op jit(solution)/shard_map/reduce_scatter | solution.py:29
  28.3 6.2 %copy-start.4 = (s32[1,1,16]{2,1,0:T(1,128)S(1)}, s32[1,1,16]{2,1,0:T(1,128)}, u32[]{:S(2)}) copy-start(s32[1,1,16]{2,1,0:T(1,128)} %param.11) | copy-start | bytes 196
  38.3 40.6 %copy-start.1 = (bf16[512,512]{1,0:T(8,128)(2,1)S(1)}, bf16[512,512]{1,0:T(8,128)(2,1)}, u32[]{:S(2)}) copy-start(bf16[512,512]{1,0:T(8,128)(2,1)} %param.14) | copy-start | bytes 1572868
  38.3 41.7 %copy-start.2 = (bf16[512,512]{1,0:T(8,128)(2,1)S(1)}, bf16[512,512]{1,0:T(8,128)(2,1)}, u32[]{:S(2)}) copy-start(bf16[512,512]{1,0:T(8,128)(2,1)} %param.15) | copy-start | bytes 1572868
  39.6 41.6 %copy-start.5 = (f32[512]{0:T(512)S(1)}, f32[512]{0:T(512)}, u32[]{:S(2)}) copy-start(f32[512]{0:T(512)} %param.16) | copy-start | bytes 6148
  80.0 3.8 %copy-start.3 = (bf16[128,512]{1,0:T(8,128)(2,1)S(1)}, bf16[128,512]{1,0:T(8,128)(2,1)}, u32[]{:S(2)}) copy-start(bf16[128,512]{1,0:T(8,128)(2,1)} %reduce-scatter.2.cloned.1.call-done) | copy-start | bytes 393220
Sparse Core Ops, SparseCore 0:
  39.7 39.0 reduce-scatter.1
where the time goes:
time: 163 us; the launch traced here: 162 us
  blocking collectives  86 us (53%)
  waiting for transfers between devices  39.3 us (24%)
  between operations  14.8 us (9%)
  matrix products  11.8 us (7%)
  local copies, waits for them, and re-layouts  8.12 us (5%)
  other arithmetic  2.3 us (1%)
    psum x1, blocking collectives, body(): grad_msg, grad_self = lax.psum((grad_msg, grad_self), ('wide', 'loop'))  61.4 us
    reduce_scatter x1, waiting for transfers between devices, body(): lax.psum_scatter(partial_value.astype(jnp.bfloat16), 'wide', scatter_dime...  39.3 us
    all_gather x1, blocking collectives, body(): gathered = lax.all_gather(own_blocks, 'loop', axis=0, tiled=True)  15.3 us
    all_gather x1, blocking collectives, body(): out_logits = lax.all_gather(logits, 'wide', axis=0, tiled=True)  9.29 us
    dot_general x1, local copies, waits for them, and re-layouts, body(): jnp.einsum('sij,sjd->sid', tile_vals, chosen, preferred_element_type=jnp....  5.52 us
    dot_general x1, matrix products, body(): jnp.einsum('sr,sid->rid', placing, product, precision=lax.Precision.HIGHEST)  3.76 us
  transfers between devices with their start and end apart: 1, of which 1 were waited for; matrix products, arithmetic and copies ran while one was open for 0% of the time, Pallas kernels for 0%

commit v1 on v0

v1 whole, which is shorter than its diff:
```python
import functools

import jax
import jax.numpy as jnp
from jax import lax
from jax.experimental import pallas as pl
from jax.experimental.pallas import tpu as pltpu
from jax.sharding import PartitionSpec as P

CHUNKS = 2
ROW_STEP = 32


def kernel(
    nl, nw, ns, tb,
    feats, tiles, t_rows, t_cols, t_count, w_msg, w_self, readout, labels,
    out_logits, out_grads,
    gath, tiles_v, nf_v, wm_v, ws_v, adj, part, sib_in, plane_out, plane_in, pre, trans,
    g_part, g_sib, g_out, g_in, z_out, z_in, lg_buf,
    local_sem, send_sem, ga_sem, rs_sib_sem, rs_pl_sem, g_sib_sem, g_pl_sem, zr_sem, za_sem,
    ap_sem, as_sem, lg_sem,
):
    f32, bf16 = jnp.float32, jnp.bfloat16
    rows_dev, width = feats.shape
    nb = rows_dev // tb
    nch = nw // 2
    share = rows_dev // nw
    gshare = 2 * width // nw
    cw = width // CHUNKS
    pieces = z_in.shape[2] and gshare // z_in.shape[2]
    prow = z_in.shape[2]
    w = lax.axis_index("wide")
    l = lax.axis_index("loop")
    core = lax.rem(w, 2)
    chip = lax.div(w, 2)
    other = 1 - core
    sib = chip * 2 + other

    def cols(c):
        return pl.ds(c * cw, cw)

    locs = [
        pltpu.make_async_copy(tiles, tiles_v, local_sem.at[0]),
        pltpu.make_async_copy(
            feats.at[pl.ds(pl.multiple_of(w * share, share), share)], nf_v, local_sem.at[1]
        ),
        pltpu.make_async_copy(w_self, ws_v, local_sem.at[2]),
        pltpu.make_async_copy(w_msg, wm_v, local_sem.at[3]),
    ]
    own_rows = pl.ds(pl.multiple_of(lax.rem(w, nb) * tb, tb), tb)
    own_copies = []
    for c in range(CHUNKS):
        own_copies.append(pltpu.make_async_copy(
            feats.at[own_rows, cols(c)],
            gath.at[c, pl.ds(pl.multiple_of(l * tb, tb), tb)],
            local_sem.at[4 + c],
        ))
    for cp in locs + own_copies:
        cp.start()

    barrier = pltpu.get_barrier_semaphore()
    for d in range(1, nw):
        pl.semaphore_signal(barrier, inc=1, device_id={"wide": lax.rem(w + d, nw), "loop": l},
                            device_id_type=pl.DeviceIdType.MESH)
    for d in range(1, nl):
        pl.semaphore_signal(barrier, inc=1, device_id={"wide": w, "loop": lax.rem(l + d, nl)},
                            device_id_type=pl.DeviceIdType.MESH)
    pl.semaphore_wait(barrier, nw + nl - 2)

    sent = []

    def send(src, dst, recv, wide, loop):
        cp = pltpu.make_async_remote_copy(
            src_ref=src, dst_ref=dst, send_sem=send_sem.at[len(sent)], recv_sem=recv,
            device_id={"wide": wide, "loop": loop}, device_id_type=pl.DeviceIdType.MESH,
        )
        cp.start()
        sent.append(cp)
        return cp

    def chip_at(e):
        return lax.rem(chip + e + nch, nch)

    def loop_at(d):
        return lax.rem(l + d + nl, nl)

    ga = []
    for c in range(CHUNKS):
        ga.append([
            send(feats.at[own_rows, cols(c)],
                 gath.at[c, pl.ds(pl.multiple_of(l * tb, tb), tb)],
                 ga_sem.at[c, d - 1], w, loop_at(d))
            for d in range(1, nl)
        ])

    locs[0].wait()
    cell = [
        jnp.where(s < t_count[0], t_rows[s] * nl + t_cols[s], -1) for s in range(ns)
    ]
    group = 4
    steps = tb // ROW_STEP

    def densify(i, carry):
        r = lax.div(i, steps)
        h = lax.rem(i, steps)
        first = r * tb + h * ROW_STEP
        share_id = lax.div(first, share)
        at = lax.div(share_id, 2) * share + lax.rem(first, share)
        for q0 in range(0, nl, group):
            accs = [jnp.zeros((ROW_STEP, tb), f32) for _ in range(group)]
            for s in range(ns):
                t = tiles_v[s, pl.ds(pl.multiple_of(h * ROW_STEP, ROW_STEP), ROW_STEP), :].astype(f32)
                for g in range(group):
                    on = jnp.where(cell[s] == r * nl + q0 + g, 1.0, 0.0).astype(f32)
                    accs[g] = accs[g] + on * t
            for g in range(group):
                adj[lax.rem(share_id, 2), pl.ds(pl.multiple_of(at, ROW_STEP), ROW_STEP),
                    pl.ds((q0 + g) * tb, tb)] = accs[g].astype(bf16)
        return carry

    lax.fori_loop(0, nb * steps, densify, 0)

    locs[1].wait()
    locs[2].wait()
    nf = nf_v[...]
    pre[...] = jnp.dot(nf, ws_v[...], preferred_element_type=f32)

    def put_trans(first, block):
        for k in range(block.shape[0] // gshare):
            j = first // gshare + k
            trans[j % 2, pl.ds((j // 2) * gshare, gshare), :] = block[k * gshare:(k + 1) * gshare]

    put_trans(width, nf.astype(f32).T.astype(bf16))
    label_col = jnp.broadcast_to(
        labels[pl.ds(w, 1), :].astype(f32), (128, share)).T[:, :1]

    sib_cp = []
    for c in range(CHUNKS):
        own_copies[c].wait()
        for cp in ga[c]:
            cp.wait_recv()
        part[c, other] = jnp.dot(adj[other], gath[c], preferred_element_type=f32).astype(bf16)
        sib_cp.append(send(part.at[c, other], sib_in.at[c], rs_sib_sem.at[c], sib, l))
        part[c, core] = jnp.dot(adj[core], gath[c], preferred_element_type=f32).astype(bf16)

    def pair_sum(c, mine, theirs, out):
        out[c] = (mine[c, core].astype(f32) + theirs[c].astype(f32)).astype(bf16)

    def spread(c, out, land, sems, size):
        return [
            send(out.at[c, pl.ds(pl.multiple_of(chip_at(e) * size, size), size)],
                 land.at[c, e - 1], sems.at[c, e - 1], chip_at(e) * 2 + core, l)
            for e in range(1, nch)
        ]

    def total(c, out, land, size):
        acc = out[c, pl.ds(pl.multiple_of(chip * size, size), size), :].astype(f32)
        for e in range(1, nch):
            acc = acc + land[c, e - 1].astype(f32)
        return acc

    pl_cp = []
    for c in range(CHUNKS):
        sib_cp[c].wait_recv()
        pair_sum(c, part, sib_in, plane_out)
        pl_cp.append(spread(c, plane_out, plane_in, rs_pl_sem, share))
    locs[3].wait()
    for c in range(CHUNKS):
        for cp in pl_cp[c]:
            cp.wait_recv()
        msg = total(c, plane_out, plane_in, share).astype(bf16)
        pre[...] += jnp.dot(msg, wm_v[pl.ds(c * cw, cw), :], preferred_element_type=f32)
        put_trans(c * cw, msg.astype(f32).T.astype(bf16))

    act = pre[...]
    gate = jax.nn.sigmoid(act)
    ro = readout[...]
    hidden = nf_v[...].astype(f32) + act * gate
    logit = jnp.sum(hidden * ro, axis=1, keepdims=True)
    resid = jax.nn.sigmoid(logit) - label_col
    pg = (resid * ro * gate * (1.0 + act * (1.0 - gate))).astype(bf16)

    sib_cp = []
    for c in range(CHUNKS):
        pgc = pg[:, c * cw:(c + 1) * cw]
        g_part[c, other] = jnp.dot(trans[other], pgc, preferred_element_type=f32).astype(bf16)
        sib_cp.append(send(g_part.at[c, other], g_sib.at[c], g_sib_sem.at[c], sib, l))
        g_part[c, core] = jnp.dot(trans[core], pgc, preferred_element_type=f32).astype(bf16)

    lg_buf[w] = jnp.broadcast_to(logit, (share, 128)).T[:8, :]

    pl_cp = []
    for c in range(CHUNKS):
        sib_cp[c].wait_recv()
        pair_sum(c, g_part, g_sib, g_out)
        pl_cp.append(spread(c, g_out, g_in, g_pl_sem, gshare))
    lg_cp = [send(lg_buf.at[w], lg_buf.at[w], lg_sem.at[d - 1], lax.rem(w + d, nw), l)
             for d in range(1, nw)]

    zr_cp = []
    for c in range(CHUNKS):
        for cp in pl_cp[c]:
            cp.wait_recv()
        z_out[c] = total(c, g_out, g_in, gshare).astype(bf16)
        cps = []
        for d in range(1, nl):
            src = z_out.at[c]
            if pieces > 1:
                src = z_out.at[c, pl.ds(pl.multiple_of(loop_at(d) * prow, prow), prow)]
            cps.append(send(src, z_in.at[c, l], zr_sem.at[c, d - 1], w, loop_at(d)))
        zr_cp.append(cps)
        if pieces > 1:
            z_in[c, l] = z_out[c, pl.ds(pl.multiple_of(l * prow, prow), prow), :]
        else:
            z_in[c, l] = z_out[c]

    def piece(wide, d):
        at = loop_at(-d) * prow if pieces > 1 else 0
        return wide, pl.ds(pl.multiple_of(at, prow), prow)

    za_cp, ap_cp, as_cp = [], [], []

    def to_plane(c, d):
        who, rws = piece(w, d)
        ref = out_grads.at[who, rws, cols(c)]
        as_cp.append(send(ref, ref, as_sem.at[c, d, 0], sib, l))
        return [send(ref, ref, ap_sem.at[c, d, e - 1], chip_at(e) * 2 + core, l)
                for e in range(1, nch)]

    for c in range(CHUNKS):
        for cp in zr_cp[c]:
            cp.wait_recv()
        acc = z_in[c, 0].astype(f32)
        for k in range(1, nl):
            acc = acc + z_in[c, k].astype(f32)
        who, rws = piece(w, 0)
        out_grads[who, rws, cols(c)] = acc.astype(bf16)
        ref = out_grads.at[who, rws, cols(c)]
        if pieces > 1:
            za_cp.append([send(ref, ref, za_sem.at[c, d - 1], w, loop_at(d))
                          for d in range(1, nl)])
        ap_cp.append([to_plane(c, 0)])
    for d in range(1, pieces):
        for c in range(CHUNKS):
            za_cp[c][d - 1].wait_recv()
            ap_cp[c].append(to_plane(c, d))
    for d in range(pieces):
        for c in range(CHUNKS):
            for e in range(1, nch):
                ap_cp[c][d][e - 1].wait_recv()
                who, rws = piece(chip_at(-e) * 2 + core, d)
                ref = out_grads.at[who, rws, cols(c)]
                as_cp.append(send(ref, ref, as_sem.at[c, d, e], sib, l))

    for cp in lg_cp:
        cp.wait_recv()
    for k in range(nw):
        out_logits[pl.ds(k, 1), :] = lg_buf[k, :1, :]
    for cp in as_cp:
        cp.wait_recv()
    for cp in sent:
        cp.wait_send()


def body(feats, tiles, tile_rows, tile_cols, tile_count, w_msg, w_self, readout, labels):
    rows_dev, width = feats.shape
    tb = tiles.shape[-1]
    ns = tiles.shape[2]
    nw, nl = lax.axis_size("wide"), lax.axis_size("loop")
    nch = nw // 2
    share = rows_dev // nw
    gshare = 2 * width // nw
    cw = width // CHUNKS
    prow = gshare // nl
    if prow < 16:
        prow = gshare
    pieces = gshare // prow
    bf16, f32 = jnp.bfloat16, jnp.float32
    sends = (
        3 * CHUNKS * (nl - 1) + 2 * CHUNKS + 2 * CHUNKS * (nch - 1) + nw - 1
        + CHUNKS * pieces * (nch - 1) + CHUNKS * pieces * nch
    )
    vmem = pl.BlockSpec(memory_space=pltpu.VMEM)
    smem = pl.BlockSpec(memory_space=pltpu.SMEM)
    hbm = pl.BlockSpec(memory_space=pl.ANY)
    dma = pltpu.SemaphoreType.DMA
    logits, grads = pl.pallas_call(
        functools.partial(kernel, nl, nw, ns, tb),
        out_shape=(
            jax.ShapeDtypeStruct((nw, share), f32),
            jax.ShapeDtypeStruct((nw, gshare, width), bf16),
        ),
        in_specs=[hbm, hbm, smem, smem, smem, hbm, hbm, vmem, vmem],
        out_specs=(vmem, vmem),
        scratch_shapes=[
            pltpu.VMEM((CHUNKS, nl * tb, cw), bf16),
            pltpu.VMEM((ns, tb, tb), bf16),
            pltpu.VMEM((share, width), bf16),
            pltpu.VMEM((width, width), bf16),
            pltpu.VMEM((width, width), bf16),
            pltpu.VMEM((2, nch * share, nl * tb), bf16),
            pltpu.VMEM((CHUNKS, 2, nch * share, cw), bf16),
            pltpu.VMEM((CHUNKS, nch * share, cw), bf16),
            pltpu.VMEM((CHUNKS, nch * share, cw), bf16),
            pltpu.VMEM((CHUNKS, nch - 1, share, cw), bf16),
            pltpu.VMEM((share, width), f32),
            pltpu.VMEM((2, nch * gshare, share), bf16),
            pltpu.VMEM((CHUNKS, 2, nch * gshare, cw), bf16),
            pltpu.VMEM((CHUNKS, nch * gshare, cw), bf16),
            pltpu.VMEM((CHUNKS, nch * gshare, cw), bf16),
            pltpu.VMEM((CHUNKS, nch - 1, gshare, cw), bf16),
            pltpu.VMEM((CHUNKS, gshare, cw), bf16),
            pltpu.VMEM((CHUNKS, nl, prow, cw), bf16),
            pltpu.VMEM((nw, 8, share), f32),
            dma((4 + CHUNKS,)),
            dma((sends,)),
            dma((CHUNKS, nl - 1)),
            dma((CHUNKS,)),
            dma((CHUNKS, nch - 1)),
            dma((CHUNKS,)),
            dma((CHUNKS, nch - 1)),
            dma((CHUNKS, nl - 1)),
            dma((CHUNKS, nl - 1)),
            dma((CHUNKS, pieces, nch - 1)),
            dma((CHUNKS, pieces, nch)),
            dma((nw - 1,)),
        ],
        compiler_params=pltpu.CompilerParams(
            collective_id=0, has_side_effects=True, vmem_limit_bytes=40 * 2**20
        ),
    )(
        feats, tiles.reshape(ns, tb, tb), tile_rows.reshape(ns), tile_cols.reshape(ns),
        tile_count.reshape(1), w_msg, w_self, readout.reshape(1, width),
        labels.reshape(nw, share),
    )
    both = grads.reshape(2, width, width)
    return logits.reshape(rows_dev), both[0], both[1]


def solution(mesh):
    placed = (
        P("loop", None),
        P("loop", "wide", None, None, None),
        P("loop", "wide", None),
        P("loop", "wide", None),
        P("loop", "wide"),
        P(),
        P(),
        P(),
        P("loop"),
    )
    return jax.shard_map(
        body, mesh=mesh, in_specs=placed, out_specs=(P("loop"), P(), P()), check_vma=False
    )
```

time: 163 us -> 60.5 us (0.37)
  blocking collectives: 86 us -> 0 us
  Pallas kernels: 0 us -> 52.2 us
  waiting for transfers between devices: 39.3 us -> 0 us
  between operations: 14.8 us -> 1.33 us
  matrix products: 11.8 us -> 0 us
  other arithmetic: 2.3 us -> 0 us
    psum x1 -> x0, blocking collectives: 61.4 us -> none  [body(): grad_msg, grad_self = lax.psum((grad_msg, grad_self), ('wide', 'loop'))]
    pallas_call x0 -> x1, Pallas kernels: none -> 52.2 us  [body(): pl.pallas_call(functools.partial(kernel, nl, nw, ns, tb), out_shape=(jax....]
    reduce_scatter x1 -> x0, waiting for transfers between devices: 39.3 us -> none  [body(): lax.psum_scatter(partial_value.astype(jnp.bfloat16), 'wide', scatter_dime...]
    all_gather x2 -> x0, blocking collectives: 24.6 us -> none  [the longest x1 15.3 us: body(): gathered = lax.all_gather(own_blocks, 'loop', axis=0, tiled=True)]
    dot_general x7 -> x0, matrix products: 11.8 us -> none  [the longest x1 3.76 us: body(): jnp.einsum('sr,sid->rid', placing, product, precision=lax.Precision.HIGHEST)]
    dot_general x1 -> x0, local copies, waits for them, and re-layouts: 5.52 us -> none  [body(): jnp.einsum('sij,sjd->sid', tile_vals, chosen, preferred_element_type=jnp....]
    unnamed x13 -> x17, local copies, waits for them, and re-layouts: 0.63 us -> 5.61 us
  transfers between devices with their start and end apart: 1 -> 0, of which waited for: 1 -> 0; matrix products, arithmetic and copies ran while one was open for 0% -> 0% of each run, Pallas kernels for 0% -> 0%
where the time goes in v1:
time: 60.5 us; the launch traced here: 60.2 us
  Pallas kernels  52.2 us (86%)
  local copies, waits for them, and re-layouts  6.65 us (11%)
  between operations  1.33 us (2%)
    pallas_call x1, Pallas kernels, body(): pl.pallas_call(functools.partial(kernel, nl, nw, ns, tb), out_shape=(jax....  52.2 us
    unnamed x17, local copies, waits for them, and re-layouts  5.61 us

profile of v1, /device:TPU:1, one launch (start us, length us, event | category | flops | bytes accessed | tf_op | source)
XLA Modules:
  0.0 60.2 jit_solution(17728737153802489636)
XLA Ops:
  1.3 0.0 copy-start.4
  1.3 0.0 copy-start.5
  1.3 0.0 copy-start.6
  1.3 0.0 copy-start.7
  1.3 0.6 %copy-done.4 = s32[1024]{0:T(1024)S(1)} copy-done((s32[1024]{0:T(1024)S(1)}, s32[1024]{0:T(1024)}, u32[]{:S(2)}) %copy-start.4) | copy-done | bytes 4120
  2.0 0.0 copy-done.5
  2.0 0.0 copy-done.6
  2.0 0.0 copy-done.7
  2.0 0.0 copy-start
  2.0 1.2 %copy-done = bf16[1024,512]{1,0:T(8,128)(2,1)S(1)} copy-done((bf16[1024,512]{1,0:T(8,128)(2,1)S(1)}, bf16[1024,512]{1,0:T(8,128)(2,1)}, u32[]{:S(2)}) %copy-start) | copy-done | bytes 1048600
  3.2 0.0 copy-start.1
  3.2 1.0 %copy-done.1 = bf16[1,1,16,128,128]{4,3,2,1,0:T(8,128)(2,1)S(1)} copy-done((bf16[1,1,16,128,128]{4,3,2,1,0:T(8,128)(2,1)S(1)}, bf16[1,1,16,128,128]{4,3,2,1,0:T(8,128)(2,1)}, u32[]{:S(2)}) %copy-start.1) | copy-done | bytes 524312
  4.3 0.0 copy-start.2
  4.3 1.0 %copy-done.2 = bf16[512,512]{1,0:T(8,128)(2,1)S(1)} copy-done((bf16[512,512]{1,0:T(8,128)(2,1)S(1)}, bf16[512,512]{1,0:T(8,128)(2,1)}, u32[]{:S(2)}) %copy-start.2) | copy-done | bytes 524312
  5.3 0.0 copy-start.3
  5.3 1.0 %copy-done.3 = bf16[512,512]{1,0:T(8,128)(2,1)S(1)} copy-done((bf16[512,512]{1,0:T(8,128)(2,1)S(1)}, bf16[512,512]{1,0:T(8,128)(2,1)}, u32[]{:S(2)}) %copy-start.3) | copy-done | bytes 524312
  6.3 52.2 %shard_map.112 = (f32[8,128]{1,0:T(8,128)S(1)}, bf16[8,128,512]{2,1,0:T(8,128)(2,1)S(1)}) custom-call(bf16[1024,512]{1,0:T(8,128)(2,1)S(1)} %copy-done, bf16[16,128,128]{2,1,0:T(8,128)(2,1)S(1)} %bitcast.10, s32[16]{0:T(128)S(1)} %bitcast.14, s32[16]{0:T(128)S(1)} %bitcast.15, s32[1]{0:T(128)} %bitcast.9.t_count, bf16[512,512]{1,0:T(8,128)(2,1)S(1)} %copy-done.2, ...), custom_call_target="tpu_custom_call" | custom-call | tf_op jit(solution)/shard_map/pallas_call | solution.py:287
  58.6 1.0 %fusion = (bf16[4,128,512]{2,1,0:T(8,128)(2,1)}, bf16[4,128,512]{2,1,0:T(8,128)(2,1)}) fusion(bf16[8,128,512]{2,1,0:T(8,128)(2,1)S(1)} %get-tuple-element.6), kind=kLoop, calls=%fused_computation | loop fusion | bytes 2097152 | tf_op jit(solution)/shard_map/slice | solution.py:337
  59.6 0.6 copy.14
Async XLA Ops:
  1.3 0.7 %copy-start.4 = (s32[1024]{0:T(1024)S(1)}, s32[1024]{0:T(1024)}, u32[]{:S(2)}) copy-start(s32[1024]{0:T(1024)} %param.17) | copy-start | bytes 12292
  1.3 0.7 %copy-start.5 = (f32[512]{0:T(512)S(1)}, f32[512]{0:T(512)}, u32[]{:S(2)}) copy-start(f32[512]{0:T(512)} %param.16) | copy-start | bytes 6148
  1.3 0.7 %copy-start.6 = (s32[1,1,16]{2,1,0:T(1,128)S(1)}, s32[1,1,16]{2,1,0:T(1,128)}, u32[]{:S(2)}) copy-start(s32[1,1,16]{2,1,0:T(1,128)} %param.11) | copy-start | bytes 196
  1.3 0.7 %copy-start.7 = (s32[1,1,16]{2,1,0:T(1,128)S(1)}, s32[1,1,16]{2,1,0:T(1,128)}, u32[]{:S(2)}) copy-start(s32[1,1,16]{2,1,0:T(1,128)} %param.12) | copy-start | bytes 196
  2.0 1.2 %copy-start = (bf16[1024,512]{1,0:T(8,128)(2,1)S(1)}, bf16[1024,512]{1,0:T(8,128)(2,1)}, u32[]{:S(2)}) copy-start(bf16[1024,512]{1,0:T(8,128)(2,1)} %feats.1) | copy-start | bytes 3145732
  3.2 1.0 %copy-start.1 = (bf16[1,1,16,128,128]{4,3,2,1,0:T(8,128)(2,1)S(1)}, bf16[1,1,16,128,128]{4,3,2,1,0:T(8,128)(2,1)}, u32[]{:S(2)}) copy-start(bf16[1,1,16,128,128]{4,3,2,1,0:T(8,128)(2,1)} %param.10) | copy-start | bytes 1572868
  4.3 1.0 %copy-start.2 = (bf16[512,512]{1,0:T(8,128)(2,1)S(1)}, bf16[512,512]{1,0:T(8,128)(2,1)}, u32[]{:S(2)}) copy-start(bf16[512,512]{1,0:T(8,128)(2,1)} %w_msg.1) | copy-start | bytes 1572868
  5.3 1.0 %copy-start.3 = (bf16[512,512]{1,0:T(8,128)(2,1)S(1)}, bf16[512,512]{1,0:T(8,128)(2,1)}, u32[]{:S(2)}) copy-start(bf16[512,512]{1,0:T(8,128)(2,1)} %w_self.1) | copy-start | bytes 1572868
